TPU v7x, 32 devices: a whole 2x2x4 slice. The times are simulated.
32 devices in a mesh: rows: 8 (over z, core), cols: 4 (over y, x).
Axes of the slice: x: 2, y: 2, z: 4, core: 2. Of those that a mesh axis runs over, the one named last changes fastest.
Arguments:
- scalar: float32 [16, 256, 2048], P(None, 'rows', 'cols'), may hold values from -6 to 6
- diffusivity: float32 [16, 256, 2048], P(None, 'rows', 'cols'), may hold values from 0.05 to 0.5
- vel_modes: float32 [6, 32, 256], P(None, 'rows', 'cols'), may hold values from -8 to 8
- offsets: int32 [256], P('rows'), may hold values from -1 to 1
Outputs:
- advanced: float32 [16, 256, 2048], P(None, 'rows', 'cols')
All inputs are finite; a program needn't handle non-finite values.
Results may differ from a plain program's by a relative error of at most 0.00007.
Values sent between devices are 32-bit elements; how exact they have to be, the bound alone decides.
A program may use at most 64 MiB of HBM per device.

v0:
```python
import functools

import jax
import jax.numpy as jnp
import numpy as np
from jax import lax
from jax.experimental import pallas as pl
from jax.experimental.pallas import tpu as pltpu
from jax.sharding import PartitionSpec as P

TIME_STEP = 0.25
RATIO = 8
HALO = 8
LANES = 128
SUB = 8
MESH = pl.DeviceIdType.MESH
HIGHEST = lax.Precision.HIGHEST


def tables(count, modes_dev, cols_dev, planes, coarse_planes, coarse_rows):
    length = count * modes_dev
    coarse_cols = cols_dev // RATIO
    tiles = cols_dev // LANES + 1
    width = tiles * LANES

    def turn(product):
        return 2.0 * np.pi * (product % length) / length

    wavenum = np.arange(length).reshape(count, modes_dev)
    first = turn(np.arange(count)[:, None, None] * coarse_cols * wavenum[None])
    shift = np.concatenate([np.cos(first) + np.sin(first), np.cos(first) - np.sin(first)], axis=-1)
    shift = shift * (0.5 * TIME_STEP / 12.0)
    places = np.arange(coarse_cols + 3) - 1
    local = turn(wavenum[:, :, None] * places[None, None, :])
    local = np.concatenate([np.cos(local), np.sin(local)], axis=1).reshape(2 * length, -1)
    breadth = -(-local.shape[1] // LANES) * LANES
    transform = np.zeros((2 * length, breadth))
    transform[:, : local.shape[1]] = local
    lane = np.arange(width)
    fine = np.where(lane >= width - HALO, lane - width, np.minimum(lane, cols_dev + HALO - 1))
    col_blend = np.zeros((breadth, width))
    base = fine // RATIO + 1
    share = (fine % RATIO) / RATIO
    col_blend[base, lane] += 1.0 - share
    col_blend[base + 1, lane] += share
    group = -(-coarse_planes * coarse_rows // 16) * 16
    depth = -(-9 * group // LANES) * LANES
    plane_blend = np.zeros((planes, depth))
    row_of = np.full((SUB, depth), -100.0)
    plane = np.arange(planes)
    weights = np.zeros((planes, coarse_planes))
    for p in plane:
        weights[p, p // RATIO % coarse_planes] += 1.0 - (p % RATIO) / RATIO
        weights[p, (p // RATIO + 1) % coarse_planes] += (p % RATIO) / RATIO
    for part in range(3):
        for block in range(3):
            for q in range(coarse_planes):
                for a in range(coarse_rows):
                    at = (part * 3 + block) * group + q * coarse_rows + a
                    plane_blend[:, at] = weights[:, q]
                    row_of[:, at] = block * coarse_rows + a
    as_f32 = functools.partial(np.asarray, dtype=np.float32)
    return (
        as_f32(shift),
        as_f32(transform),
        as_f32(col_blend),
        as_f32(plane_blend),
        as_f32(row_of),
    )


def parts_of(value):
    high = value.astype(jnp.bfloat16)
    rest = value - high.astype(jnp.float32)
    middle = rest.astype(jnp.bfloat16)
    low = (rest - middle.astype(jnp.float32)).astype(jnp.bfloat16)
    return high, middle, low


def kernel(
    n_rows, n_cols, chunks,
    s_hbm, k_hbm, m_hbm, off_hbm, shift_hbm, transform_hbm, blend_hbm, planes_hbm, rowof_hbm,
    o_ref,
    s_ref, k_ref, m_ref, off_ref, shift_ref, transform_ref, blend_ref, planes_ref, rowof_ref,
    load_sem,
    message, modes, packed, strips, above, below, blend_rows, speeds,
    field, kappa, state_b, state_c, state_d, coef,
    vel_send, vel_recv, strip_send, strip_recv, row_send, row_recv,
):
    planes, rows_dev, cols_dev = s_ref.shape
    own_tiles = cols_dev // LANES
    tiles = own_tiles + 1
    tall = rows_dev + 2 * HALO
    coarse = m_ref.shape[0]
    coarse_planes = coarse // 2
    coarse_rows = m_ref.shape[1]
    group = modes.shape[1] // 3 // 2 - SUB // 2
    block = 2 * group + SUB
    r = lax.axis_index("rows")
    c = lax.axis_index("cols")
    row_at = {-1: lax.rem(r + n_rows - 1, n_rows), 0: r, 1: lax.rem(r + 1, n_rows)}
    col_at = [c] + [lax.rem(c + d, n_cols) for d in range(1, n_cols)]
    left, right = col_at[n_cols - 1], col_at[1]

    loads = [
        pltpu.make_async_copy(src, dst, load_sem.at[i])
        for i, (src, dst) in enumerate((
            (m_hbm, m_ref), (off_hbm, off_ref), (s_hbm, s_ref), (k_hbm, k_ref),
            (shift_hbm, shift_ref), (transform_hbm, transform_ref), (blend_hbm, blend_ref),
            (planes_hbm, planes_ref), (rowof_hbm, rowof_ref),
        ))
    ]
    barrier = pltpu.get_barrier_semaphore()
    partners = [(dr, d) for d in range(n_cols) for dr in (-1, 0, 1) if (dr, d) != (0, 0)]
    for dr, d in partners:
        pl.semaphore_signal(barrier, inc=1, device_id=(row_at[dr], col_at[d]), device_id_type=MESH)

    for copy in loads:
        copy.start()
    message[...] = jnp.zeros_like(message)
    loads[0].wait()
    loads[1].wait()
    for part in range(coarse):
        at = part // coarse_planes * group + part % coarse_planes * coarse_rows
        once = m_ref[part]
        message[at : at + coarse_rows, :] = jnp.concatenate([once, once], axis=-1)
    message[2 * group :, 0:rows_dev] = jnp.broadcast_to(
        off_ref[...].astype(jnp.float32), (SUB, rows_dev)
    )
    pl.semaphore_wait(barrier, len(partners))

    def send(src, dst, sems, target):
        copy = pltpu.make_async_remote_copy(
            src_ref=src, dst_ref=dst, send_sem=sems[0], recv_sem=sems[1],
            device_id=target, device_id_type=MESH,
        )
        copy.start()
        return copy

    vel_copies = []
    for index, (dr, d) in enumerate(partners):
        vel_copies.append(send(
            message, modes.at[c, pl.ds((1 - dr) * block, block)],
            (vel_send.at[index], vel_recv.at[index]), (row_at[dr], col_at[d]),
        ))

    loads[2].wait()
    loads[3].wait()
    lane8 = lax.broadcasted_iota(jnp.int32, (rows_dev, LANES), 1)
    for side in range(2):
        for array, ref in enumerate((s_ref, k_ref)):
            total = jnp.zeros((rows_dev, LANES), jnp.float32)
            for p in range(planes):
                if side == 0:
                    edge = pltpu.roll(ref[p, :, 0:LANES], (HALO * p) % LANES, 1)
                else:
                    edge = pltpu.roll(ref[p, :, cols_dev - LANES :], (HALO * (p + 1)) % LANES, 1)
                total = jnp.where(lane8 // HALO == p, edge, total)
            packed[side, array] = total
    strip_copies = []
    for side, target in ((0, left), (1, right)):
        there = strips.at[1 - side]
        for index, (dr, first, extent, place) in enumerate((
            (0, 0, rows_dev, HALO),
            (-1, 0, HALO, HALO + rows_dev),
            (1, rows_dev - HALO, HALO, 0),
        )):
            at = side * 3 + index
            strip_copies.append(send(
                packed.at[side, :, pl.ds(first, extent)], there.at[:, pl.ds(place, extent)],
                (strip_send.at[at], strip_recv.at[at]), (row_at[dr], target),
            ))

    per_chunk = planes // chunks
    row_copies = []
    for chunk in range(chunks):
        mine = pl.ds(chunk * per_chunk, per_chunk)
        held = []
        for array, ref in enumerate((s_ref, k_ref)):
            at = (chunk * 2 + array) * 2
            held.append(send(
                ref.at[mine, pl.ds(0, HALO)], below.at[array, mine],
                (row_send.at[at], row_recv.at[at]), (row_at[-1], c),
            ))
            held.append(send(
                ref.at[mine, pl.ds(rows_dev - HALO, HALO)], above.at[array, mine],
                (row_send.at[at + 1], row_recv.at[at + 1]), (row_at[1], c),
            ))
        row_copies.append(held)

    modes[c, pl.ds(block, block)] = message[...]
    for copy in loads[4:]:
        copy.wait()
    for copy in vel_copies:
        copy.wait_recv()
    depth = rowof_ref.shape[1]
    offsets_at = jnp.zeros((tall, LANES), jnp.float32)
    lane = lax.broadcasted_iota(jnp.int32, (tall, LANES), 1)
    ext = lax.broadcasted_iota(jnp.int32, (tall, LANES), 0)
    for part in range(3):
        values = modes[c, part * block + 2 * group : (part + 1) * block, :][0:1]
        here = (lane == ext - HALO + rows_dev * (1 - part)) & (lane < rows_dev)
        offsets_at = offsets_at + jnp.where(here, values, 0.0)
    offset = jnp.dot(
        offsets_at, jnp.ones((LANES, depth), jnp.float32), precision=HIGHEST,
        preferred_element_type=jnp.float32,
    )
    fine = lax.broadcasted_iota(jnp.int32, (tall, depth), 0)
    base = (fine // RATIO + (coarse_rows - 1)).astype(jnp.float32) + offset
    share = (fine % RATIO).astype(jnp.float32) / RATIO
    row_of = rowof_ref[0:1, :]
    near = jnp.where(jnp.abs(row_of - base) < 0.5, 1.0 - share, 0.0) + jnp.where(
        jnp.abs(row_of - base - 1.0) < 0.5, share, 0.0
    )
    for p in range(planes):
        blend_rows[p * tall : (p + 1) * tall, :] = (near * planes_ref[p : p + 1, :]).astype(
            jnp.bfloat16
        )
    scale = shift_ref[c]
    spectrum = jnp.concatenate(
        [modes[d] * scale[d : d + 1, :] for d in range(n_cols)], axis=-1
    )
    physical = jnp.dot(
        spectrum, transform_ref[...], precision=HIGHEST, preferred_element_type=jnp.float32
    )
    blend = blend_ref[...].astype(jnp.bfloat16)
    along = sum(
        jnp.dot(part, blend, preferred_element_type=jnp.float32)
        for part in reversed(parts_of(physical))
    )
    for m in range(2):
        picked = jnp.concatenate(
            [along[b * block + m * group : b * block + (m + 1) * group] for b in range(3)], axis=0
        )
        stack = list(parts_of(picked))
        short = depth - 9 * group
        if short:
            stack.append(jnp.zeros((short, picked.shape[1]), jnp.bfloat16))
        stacked = jnp.concatenate(stack, axis=0)
        for t in range(0, tiles, 2):
            wide = min(2, tiles - t)
            speed = jnp.dot(
                blend_rows[...], stacked[:, t * LANES : (t + wide) * LANES],
                preferred_element_type=jnp.float32,
            )
            for n in range(wide):
                speeds[m, t + n] = speed[:, n * LANES : (n + 1) * LANES].reshape(
                    planes, tall, LANES
                )

    for copy in strip_copies:
        copy.wait_recv()

    lane1 = lax.broadcasted_iota(jnp.int32, (SUB, LANES), 1)
    from_right = {k: lane1 < LANES - k for k in (1, 2)}
    from_left = {k: lane1 >= k for k in (1, 2)}
    halo_lane = lax.broadcasted_iota(jnp.int32, (tall, LANES), 1) < HALO

    def shifted(values, k):
        rolled = [pltpu.roll(v, (LANES - k) % LANES, 1) for v in values]
        if k > 0:
            return [
                jnp.where(from_right[k], rolled[t], rolled[(t + 1) % tiles]) for t in range(tiles)
            ]
        return [jnp.where(from_left[-k], rolled[t], rolled[t - 1]) for t in range(tiles)]

    def rows_of(ref, at, step=0):
        first = SUB + at + step
        return [ref[t, first : first + SUB, :] for t in range(tiles)]

    def tendency(ref, at):
        centre = rows_of(ref, at)
        ups, downs = rows_of(ref, at, 1), rows_of(ref, at, -1)
        ups2, downs2 = rows_of(ref, at, 2), rows_of(ref, at, -2)
        r1, l1, r2, l2 = (shifted(centre, k) for k in (1, -1, 2, -2))
        result = []
        for t in range(tiles):
            w = [coef[n, t, at : at + SUB, :] for n in range(7)]
            rows = w[0] * ups[t] + w[1] * downs[t] + w[5] * (ups2[t] - downs2[t])
            cols = w[2] * r1[t] + w[3] * l1[t] + w[6] * (r2[t] - l2[t])
            result.append((rows + cols) - w[4] * centre[t])
        return result

    def one_plane(p, carry):
        for array, (ref, work, gain) in enumerate(
            ((s_ref, field, None), (k_ref, kappa, 0.25 * TIME_STEP))
        ):
            def put(value):
                return value if gain is None else value * gain

            for t in range(own_tiles):
                at = slice(t * LANES, (t + 1) * LANES)
                work[t, SUB : SUB + HALO, :] = put(above[array, p, :, at])
                work[t, SUB + HALO : SUB + HALO + rows_dev, :] = put(ref[p, :, at])
                work[t, SUB + HALO + rows_dev : SUB + tall, :] = put(below[array, p, :, at])
            from_l = pltpu.roll(strips[0, array], lax.rem(2 * LANES - HALO * (p + 1), LANES), 1)
            from_r = pltpu.roll(strips[1, array], lax.rem(LANES - HALO * p, LANES), 1)
            work[own_tiles, SUB : SUB + tall, :] = put(jnp.where(halo_lane, from_r, from_l))

        for at in range(0, tall, SUB):
            centre = rows_of(kappa, at)
            ups, downs = rows_of(kappa, at, 1), rows_of(kappa, at, -1)
            rights, lefts = shifted(centre, 1), shifted(centre, -1)
            for t in range(tiles):
                u = speeds[0, t, p, at : at + SUB, :]
                v = speeds[1, t, p, at : at + SUB, :]
                u8, v8 = 8.0 * u, 8.0 * v
                east = centre[t] + ups[t] - u8
                west = centre[t] + downs[t] + u8
                north = centre[t] + rights[t] - v8
                south = centre[t] + lefts[t] + v8
                for n, value in enumerate(
                    (east, west, north, south, (east + west) + (north + south), u, v)
                ):
                    coef[n, t, at : at + SUB, :] = value

        for src, dst, span, gain in (
            (field, state_b, (0, tall), 1.0),
            (state_b, state_c, (4, tall - 4), 1.0),
            (state_c, state_d, (4, tall - 4), 2.0),
        ):
            for at in range(*span, SUB):
                slope = tendency(src, at)
                start = rows_of(field, at)
                for t in range(tiles):
                    dst[t, SUB + at : 2 * SUB + at, :] = start[t] + (
                        slope[t] if gain == 1.0 else gain * slope[t]
                    )
        for at in range(HALO, HALO + rows_dev, SUB):
            slope = tendency(state_d, at)
            a, b = rows_of(field, at), rows_of(state_b, at)
            e, g = rows_of(state_c, at), rows_of(state_d, at)
            for t in range(own_tiles):
                sums = (b[t] - a[t]) + 2.0 * e[t] + (g[t] + slope[t])
                o_ref[p, at - HALO : at - HALO + SUB, t * LANES : (t + 1) * LANES] = sums * (
                    1.0 / 3.0
                )
        return carry

    for chunk in range(chunks):
        for copy in row_copies[chunk]:
            copy.wait_recv()
        lax.fori_loop(chunk * per_chunk, (chunk + 1) * per_chunk, one_plane, 0)

    for copy in vel_copies + strip_copies + sum(row_copies, []):
        copy.wait_send()


def solution(mesh):
    n_rows, n_cols = mesh.shape["rows"], mesh.shape["cols"]
    chunks = 4

    def per_device(scalar, diffusivity, vel_modes, offsets):
        planes, rows_dev, cols_dev = scalar.shape
        coarse, coarse_rows, modes_dev = vel_modes.shape
        consts = tables(n_cols, modes_dev, cols_dev, planes, coarse // 2, coarse_rows)
        tiles = cols_dev // LANES + 1
        tall = rows_dev + 2 * HALO
        group = -(-(coarse // 2 * coarse_rows) // 16) * 16
        block = 2 * group + SUB
        depth = consts[4].shape[1]
        partners = 3 * n_cols - 1
        work = pltpu.VMEM((tiles, tall + 2 * SUB, LANES), jnp.float32)
        dma = pltpu.SemaphoreType.DMA
        operands = (scalar, diffusivity, vel_modes, offsets.reshape(1, rows_dev), *consts)
        return pl.pallas_call(
            functools.partial(kernel, n_rows, n_cols, chunks),
            out_shape=jax.ShapeDtypeStruct(scalar.shape, jnp.float32),
            in_specs=[pl.BlockSpec(memory_space=pl.ANY)] * len(operands),
            out_specs=pl.BlockSpec(memory_space=pltpu.VMEM),
            scratch_shapes=[pltpu.VMEM(x.shape, x.dtype) for x in operands] + [
                dma((len(operands),)),
                pltpu.VMEM((block, 2 * modes_dev), jnp.float32),
                pltpu.VMEM((n_cols, 3 * block, 2 * modes_dev), jnp.float32),
                pltpu.VMEM((2, 2, rows_dev, LANES), jnp.float32),
                pltpu.VMEM((2, 2, tall, LANES), jnp.float32),
                pltpu.VMEM((2, planes, HALO, cols_dev), jnp.float32),
                pltpu.VMEM((2, planes, HALO, cols_dev), jnp.float32),
                pltpu.VMEM((planes * tall, depth), jnp.bfloat16),
                pltpu.VMEM((2, tiles, planes, tall, LANES), jnp.float32),
                work, work, work, work, work,
                pltpu.VMEM((7, tiles, tall, LANES), jnp.float32),
                dma((partners,)), dma((partners,)),
                dma((6,)), dma((6,)),
                dma((4 * chunks,)), dma((4 * chunks,)),
            ],
            compiler_params=pltpu.CompilerParams(
                collective_id=0, has_side_effects=True, vmem_limit_bytes=56 * 1024 * 1024
            ),
        )(*operands)

    return jax.shard_map(
        per_device,
        mesh=mesh,
        in_specs=(
            P(None, "rows", "cols"),
            P(None, "rows", "cols"),
            P(None, "rows", "cols"),
            P("rows"),
        ),
        out_specs=P(None, "rows", "cols"),
        check_vma=False,
    )
```

profile of v0, /device:TPU:0, one launch (start us, length us, event | category | flops | bytes accessed | tf_op | source)
XLA Modules:
  0.0 28.0 jit_solution(15427921628247573148)
XLA Ops:
  0.0 25.7 %shard_map.91 = f32[16,32,512]{2,1,0:T(8,128)} custom-call(f32[16,32,512]{2,1,0:T(8,128)} %s_hbm.1, f32[16,32,512]{2,1,0:T(8,128)} %k_hbm.1, f32[6,4,64]{2,1,0:T(4,128)} %m_hbm.1, s32[1,32]{1,0:T(1,128)} %bitcast.1, f32[4,4,128]{2,1,0:T(4,128)} %constant.10.clone.shift_hbm, f32[512,128]{1,0:T(8,128)} %constant.11.clone.transform_hbm, ...), custom_call_target="tpu_custom_call" | custom-call | tf_op jit(solution)/shard_map/pallas_call | solution.py:366
  25.7 2.3 %copy.11 = f32[16,32,512]{2,1,0:T(8,128)} copy(f32[16,32,512]{2,1,0:T(8,128)} %shard_map.91) | data formatting | bytes 2097152
where the time goes:
time: 28.2 us; the launch traced here: 28 us
  Pallas kernels  25.7 us (91%)
  local copies, waits for them, and re-layouts  2.29 us (8%)
    pallas_call x1, Pallas kernels, per_device(): pl.pallas_call(functools.partial(kernel, n_rows, n_cols, chunks), out_sha...  25.7 us
    unnamed x1, local copies, waits for them, and re-layouts  2.29 us

commit v1 on v0

--- a/solution.py
+++ b/solution.py
@@ -172,21 +172,28 @@
             ))
 
     per_chunk = planes // chunks
-    row_copies = []
-    for chunk in range(chunks):
+
+    def row_copies(chunk):
         mine = pl.ds(chunk * per_chunk, per_chunk)
         held = []
         for array, ref in enumerate((s_ref, k_ref)):
             at = (chunk * 2 + array) * 2
-            held.append(send(
-                ref.at[mine, pl.ds(0, HALO)], below.at[array, mine],
-                (row_send.at[at], row_recv.at[at]), (row_at[-1], c),
-            ))
-            held.append(send(
-                ref.at[mine, pl.ds(rows_dev - HALO, HALO)], above.at[array, mine],
-                (row_send.at[at + 1], row_recv.at[at + 1]), (row_at[1], c),
-            ))
-        row_copies.append(held)
+            for side, (dr, first, there) in enumerate((
+                (-1, 0, below), (1, rows_dev - HALO, above),
+            )):
+                held.append(pltpu.make_async_remote_copy(
+                    src_ref=ref.at[mine, pl.ds(first, HALO)], dst_ref=there.at[array, mine],
+                    send_sem=row_send.at[at + side], recv_sem=row_recv.at[at + side],
+                    device_id=(row_at[dr], c), device_id_type=MESH,
+                ))
+        return held
+
+    def start_rows(chunk, carry):
+        for copy in row_copies(chunk):
+            copy.start()
+        return carry
+
+    lax.fori_loop(0, chunks, start_rows, 0)
 
     modes[c, pl.ds(block, block)] = message[...]
     for copy in loads[4:]:
@@ -202,8 +209,7 @@
         here = (lane == ext - HALO + rows_dev * (1 - part)) & (lane < rows_dev)
         offsets_at = offsets_at + jnp.where(here, values, 0.0)
     offset = jnp.dot(
-        offsets_at, jnp.ones((LANES, depth), jnp.float32), precision=HIGHEST,
-        preferred_element_type=jnp.float32,
+        offsets_at, jnp.ones((LANES, depth), jnp.float32), preferred_element_type=jnp.float32
     )
     fine = lax.broadcasted_iota(jnp.int32, (tall, depth), 0)
     base = (fine // RATIO + (coarse_rows - 1)).astype(jnp.float32) + offset
@@ -337,18 +343,26 @@
                 )
         return carry
 
-    for chunk in range(chunks):
-        for copy in row_copies[chunk]:
+    def one_chunk(chunk, carry):
+        for copy in row_copies(chunk):
             copy.wait_recv()
-        lax.fori_loop(chunk * per_chunk, (chunk + 1) * per_chunk, one_plane, 0)
-
-    for copy in vel_copies + strip_copies + sum(row_copies, []):
+        return lax.fori_loop(chunk * per_chunk, (chunk + 1) * per_chunk, one_plane, carry)
+
+    lax.fori_loop(0, chunks, one_chunk, 0)
+
+    def end_rows(chunk, carry):
+        for copy in row_copies(chunk):
+            copy.wait_send()
+        return carry
+
+    lax.fori_loop(0, chunks, end_rows, 0)
+    for copy in vel_copies + strip_copies:
         copy.wait_send()
 
 
 def solution(mesh):
     n_rows, n_cols = mesh.shape["rows"], mesh.shape["cols"]
-    chunks = 4
+    chunks = 8
 
     def per_device(scalar, diffusivity, vel_modes, offsets):
         planes, rows_dev, cols_dev = scalar.shape
@@ -385,7 +399,7 @@
                 dma((4 * chunks,)), dma((4 * chunks,)),
             ],
             compiler_params=pltpu.CompilerParams(
-                collective_id=0, has_side_effects=True, vmem_limit_bytes=56 * 1024 * 1024
+                collective_id=0, has_side_effects=True, vmem_limit_bytes=40 * 1024 * 1024
             ),
         )(*operands)
 

time: 28.2 us -> 32.4 us (1.15)
  local copies, waits for them, and re-layouts: 2.29 us -> 8.16 us
  Pallas kernels: 25.7 us -> 23.7 us
    unnamed x1 -> x19, local copies, waits for them, and re-layouts: 2.29 us -> 8.16 us
    pallas_call x1, Pallas kernels: 25.7 us -> 23.7 us  [per_device(): pl.pallas_call(functools.partial(kernel, n_rows, n_cols, chunks), out_sha...]
where the time goes in v1:
time: 32.4 us; the launch traced here: 31.9 us
  Pallas kernels  23.7 us (73%)
  local copies, waits for them, and re-layouts  8.16 us (25%)
    pallas_call x1, Pallas kernels, per_device(): pl.pallas_call(functools.partial(kernel, n_rows, n_cols, chunks), out_sha...  23.7 us
    unnamed x19, local copies, waits for them, and re-layouts  8.16 us

profile of v1, /device:TPU:0, one launch (start us, length us, event | category | flops | bytes accessed | tf_op | source)
XLA Modules:
  0.0 31.9 jit_solution(2346846059794933087)
XLA Ops:
  0.0 0.0 copy-start.6
  0.0 0.0 copy-start.8
  0.0 0.7 %copy-done.6 = f32[8,256]{1,0:T(8,128)S(1)} copy-done((f32[8,256]{1,0:T(8,128)S(1)}, f32[8,256]{1,0:T(8,128)}, u32[]{:S(2)}) %copy-start.6) | copy-done | bytes 8216
  0.7 0.0 copy-done.8
  0.7 0.0 copy-start
  0.7 1.2 %copy-done = f32[16,32,512]{2,1,0:T(8,128)S(1)} copy-done((f32[16,32,512]{2,1,0:T(8,128)S(1)}, f32[16,32,512]{2,1,0:T(8,128)}, u32[]{:S(2)}) %copy-start) | copy-done | bytes 1048600
  1.9 0.0 copy-start.1
  1.9 1.2 %copy-done.1 = f32[16,32,512]{2,1,0:T(8,128)S(1)} copy-done((f32[16,32,512]{2,1,0:T(8,128)S(1)}, f32[16,32,512]{2,1,0:T(8,128)}, u32[]{:S(2)}) %copy-start.1) | copy-done | bytes 1048600
  3.2 0.0 copy-start.2
  3.2 1.0 %copy-done.2 = f32[128,640]{1,0:T(8,128)S(1)} copy-done((f32[128,640]{1,0:T(8,128)S(1)}, f32[128,640]{1,0:T(8,128)}, u32[]{:S(2)}) %copy-start.2) | copy-done | bytes 327704
  4.1 0.0 copy-start.3
  4.1 0.9 %copy-done.3 = f32[512,128]{1,0:T(8,128)S(1)} copy-done((f32[512,128]{1,0:T(8,128)S(1)}, f32[512,128]{1,0:T(8,128)}, u32[]{:S(2)}) %copy-start.3) | copy-done | bytes 262168
  5.1 0.0 copy-start.4
  5.1 0.7 %copy-done.4 = f32[16,256]{1,0:T(8,128)S(1)} copy-done((f32[16,256]{1,0:T(8,128)S(1)}, f32[16,256]{1,0:T(8,128)}, u32[]{:S(2)}) %copy-start.4) | copy-done | bytes 16408
  5.8 0.0 copy-start.5
  5.8 0.7 %copy-done.5 = f32[6,4,64]{2,1,0:T(4,128)S(1)} copy-done((f32[6,4,64]{2,1,0:T(4,128)S(1)}, f32[6,4,64]{2,1,0:T(4,128)}, u32[]{:S(2)}) %copy-start.5) | copy-done | bytes 6168
  6.5 0.0 copy-start.7
  6.5 0.7 %copy-done.7 = f32[4,4,128]{2,1,0:T(4,128)S(1)} copy-done((f32[4,4,128]{2,1,0:T(4,128)S(1)}, f32[4,4,128]{2,1,0:T(4,128)}, u32[]{:S(2)}) %copy-start.7) | copy-done | bytes 8216
  7.2 23.7 %shard_map.91 = f32[16,32,512]{2,1,0:T(8,128)S(1)} custom-call(f32[16,32,512]{2,1,0:T(8,128)S(1)} %copy-done, f32[16,32,512]{2,1,0:T(8,128)S(1)} %copy-done.1, f32[6,4,64]{2,1,0:T(4,128)S(1)} %copy-done.5, s32[1,32]{1,0:T(1,128)S(1)} %bitcast.1, f32[4,4,128]{2,1,0:T(4,128)S(1)} %copy-done.7, f32[512,128]{1,0:T(8,128)S(1)} %copy-done.3, ...), custom_call_target="tpu_custom_call" | custom-call | tf_op jit(solution)/shard_map/pallas_call | solution.py:380
  30.9 1.0 %copy.11 = f32[16,32,512]{2,1,0:T(8,128)} copy(f32[16,32,512]{2,1,0:T(8,128)S(1)} %shard_map.91) | data formatting | bytes 2097152
Async XLA Ops:
  0.0 0.7 %copy-start.6 = (f32[8,256]{1,0:T(8,128)S(1)}, f32[8,256]{1,0:T(8,128)}, u32[]{:S(2)}) copy-start(f32[8,256]{1,0:T(8,128)} %constant.14.clone.rowof_hbm) | copy-start | bytes 24580
  0.0 0.7 %copy-start.8 = (s32[32]{0:T(128)S(1)}, s32[32]{0:T(128)}, u32[]{:S(2)}) copy-start(s32[32]{0:T(128)} %param.12) | copy-start | bytes 388
  0.7 1.2 %copy-start = (f32[16,32,512]{2,1,0:T(8,128)S(1)}, f32[16,32,512]{2,1,0:T(8,128)}, u32[]{:S(2)}) copy-start(f32[16,32,512]{2,1,0:T(8,128)} %s_hbm.1) | copy-start | bytes 3145732
  1.9 1.2 %copy-start.1 = (f32[16,32,512]{2,1,0:T(8,128)S(1)}, f32[16,32,512]{2,1,0:T(8,128)}, u32[]{:S(2)}) copy-start(f32[16,32,512]{2,1,0:T(8,128)} %k_hbm.1) | copy-start | bytes 3145732
  3.2 1.0 %copy-start.2 = (f32[128,640]{1,0:T(8,128)S(1)}, f32[128,640]{1,0:T(8,128)}, u32[]{:S(2)}) copy-start(f32[128,640]{1,0:T(8,128)} %constant.12.clone.blend_hbm) | copy-start | bytes 983044
  4.1 0.9 %copy-start.3 = (f32[512,128]{1,0:T(8,128)S(1)}, f32[512,128]{1,0:T(8,128)}, u32[]{:S(2)}) copy-start(f32[512,128]{1,0:T(8,128)} %constant.11.clone.transform_hbm) | copy-start | bytes 786436
  5.1 0.7 %copy-start.4 = (f32[16,256]{1,0:T(8,128)S(1)}, f32[16,256]{1,0:T(8,128)}, u32[]{:S(2)}) copy-start(f32[16,256]{1,0:T(8,128)} %constant.13.clone.planes_hbm) | copy-start | bytes 49156
  5.8 0.7 %copy-start.5 = (f32[6,4,64]{2,1,0:T(4,128)S(1)}, f32[6,4,64]{2,1,0:T(4,128)}, u32[]{:S(2)}) copy-start(f32[6,4,64]{2,1,0:T(4,128)} %m_hbm.1) | copy-start | bytes 18436
  6.5 0.7 %copy-start.7 = (f32[4,4,128]{2,1,0:T(4,128)S(1)}, f32[4,4,128]{2,1,0:T(4,128)}, u32[]{:S(2)}) copy-start(f32[4,4,128]{2,1,0:T(4,128)} %constant.10.clone.shift_hbm) | copy-start | bytes 24580
